TPU v7x, 32 devices: a whole 2x2x4 slice. The times are simulated.
32 devices in a mesh: groups: 2 (over y), seq: 8 (over z, x), heads: 2 (over core).
Axes of the slice: x: 2, y: 2, z: 4, core: 2. Of those that a mesh axis runs over, the one named last changes fastest.
Arguments:
- queries: bfloat16 [4096, 16, 128], P(('groups', 'seq'), 'heads'), parts along dimension 0, may hold values from -20 to 20
- keys: bfloat16 [4096, 16, 128], P(('groups', 'seq'), 'heads'), parts along dimension 0, may hold values from -18 to 18
- values: bfloat16 [4096, 16, 128], P(('groups', 'seq'), 'heads'), parts along dimension 0, may hold values from -6 to 6
- out_grad: bfloat16 [4096, 16, 128], P(('groups', 'seq'), 'heads'), parts along dimension 0, may hold values from -6 to 6
- spans: int32 [3, 4096], P(None, ('groups', 'seq')), parts along dimension 1, may hold values from 0 to 2048, as said below
Outputs:
- attended: bfloat16 [4096, 16, 128], P(('groups', 'seq'), 'heads'), parts along dimension 0
- query_grad: bfloat16 [4096, 16, 128], P(('groups', 'seq'), 'heads'), parts along dimension 0
- key_grad: bfloat16 [4096, 16, 128], P(('groups', 'seq'), 'heads'), parts along dimension 0
- value_grad: bfloat16 [4096, 16, 128], P(('groups', 'seq'), 'heads'), parts along dimension 0
There are 2 independent parts, one for each index of `groups`. A program takes and returns all parts, laid end to end along the dimension named above; each array names one. Nothing has to cross between parts.
Inputs may be any that keep to these rules, and one draw needn't show every extreme that they name: Triples lie end to end from position 0; for each token spans[0] <= position, spans[0] < spans[1] <= spans[2], and all tokens of a triple share the three values. A triple holds at most 512 tokens, and one holds exactly 512. The triple that holds the last token has spans[2] = 2048.
All inputs are finite; a program needn't handle non-finite values.
Results may differ from a plain program's by a relative error of at most 0.022.
Values may be sent and summed in bfloat16 or wider, within the bound.
A program may use at most 64 MiB of HBM per device.

v0:
```python
from functools import reduce
import math

import jax
import jax.numpy as jnp
from jax import lax
from jax.sharding import PartitionSpec as P

REACH = 2


NEG = -1e30


def from_behind(value, axis, by):
    count = lax.axis_size(axis)
    pairs = [(i, i + by) for i in range(count) if 0 <= i + by < count]
    return lax.ppermute(value, axis, pairs)


def tile_mask(query_pos, key_pos, starts, chosen, rejected):
    allowed = (key_pos[None, :] >= starts[:, None]) & (key_pos[None, :] <= query_pos[:, None])
    crossed = (
        (query_pos >= rejected)[:, None]
        & (key_pos[None, :] >= chosen[:, None])
        & (key_pos[None, :] < rejected[:, None])
    )
    return allowed & jnp.logical_not(crossed)


def masked_scores(queries, kv_tile, visible, score_scale):
    raw = (
        jnp.einsum("qhd,khd->hqk", queries, kv_tile[0], preferred_element_type=jnp.float32)
        * score_scale
    )
    return jnp.where(visible[None], raw, NEG)


def forward_part(scores, kv_tile, row_max):
    weights = jnp.exp(scores - row_max[..., None])
    mixed = jnp.einsum(
        "hqk,khd->qhd", weights.astype(jnp.bfloat16), kv_tile[1], preferred_element_type=jnp.float32
    )
    return (jnp.sum(weights, axis=-1), mixed)


def backward_part(scores, kv_tile, queries, out_grad, log_total, delta, score_scale):
    probs = jnp.exp(scores - log_total[..., None])
    value_part = jnp.einsum(
        "hqk,qhd->khd", probs.astype(jnp.bfloat16), out_grad, preferred_element_type=jnp.float32
    )
    prob_grad = jnp.einsum("qhd,khd->hqk", out_grad, kv_tile[1], preferred_element_type=jnp.float32)
    score_grad = (probs * (prob_grad - delta[..., None])).astype(jnp.bfloat16)
    query_part = jnp.einsum(
        "hqk,khd->qhd", score_grad, kv_tile[0], preferred_element_type=jnp.float32
    )
    key_part = (
        jnp.einsum("hqk,qhd->khd", score_grad, queries, preferred_element_type=jnp.float32)
        * score_scale
    )
    return (query_part, jnp.stack((key_part, value_part)))


def per_device(queries, keys, values, out_grad, spans):
    tok_rows, head_count, head_size = queries.shape
    score_scale = 1.0 / math.sqrt(head_size)
    anchor = lax.axis_index("seq") * tok_rows
    offsets = jnp.arange(tok_rows, dtype=jnp.int32)
    query_pos = anchor + offsets
    starts, chosen, rejected = (spans[0], spans[1], spans[2])
    paired = jnp.stack((keys, values))
    kv_tiles = [paired]
    for distance in range(1, REACH + 1):
        kv_tiles.append(from_behind(paired, "seq", distance))
    score_list = []
    for distance in range(REACH + 1):
        key_pos = anchor - distance * tok_rows + offsets
        visible = tile_mask(query_pos, key_pos, starts, chosen, rejected)
        kv_tile = kv_tiles[distance]
        score_list.append(
            (
                lambda kv_tile=kv_tile, visible=visible: masked_scores(
                    queries, kv_tile, visible, score_scale
                )
            )()
        )
    row_max = reduce(jnp.maximum, [jnp.max(scores, axis=-1) for scores in score_list])
    row_sum = jnp.zeros((head_count, tok_rows), jnp.float32)
    mixed_total = jnp.zeros((tok_rows, head_count, head_size), jnp.float32)
    for distance in range(REACH + 1):
        scores = score_list[distance]
        kv_tile = kv_tiles[distance]
        part_sum, part_mixed = (
            lambda scores=scores, kv_tile=kv_tile: forward_part(scores, kv_tile, row_max)
        )()
        row_sum = row_sum + part_sum
        mixed_total = mixed_total + part_mixed
    attended = (mixed_total / row_sum.T[:, :, None]).astype(jnp.bfloat16)
    log_total = row_max + jnp.log(row_sum)
    delta = jnp.sum(out_grad.astype(jnp.float32) * attended.astype(jnp.float32), axis=-1).T
    query_total = jnp.zeros((tok_rows, head_count, head_size), jnp.float32)
    grad_parts = []
    for distance in range(REACH + 1):
        scores = score_list[distance]
        kv_tile = kv_tiles[distance]
        query_part, pair_part = (
            lambda scores=scores, kv_tile=kv_tile: backward_part(
                scores, kv_tile, queries, out_grad, log_total, delta, score_scale
            )
        )()
        query_total = query_total + query_part
        grad_parts.append(pair_part)
    pair_total = grad_parts[0]
    for distance in range(1, REACH + 1):
        pair_total = pair_total + from_behind(
            grad_parts[distance].astype(jnp.bfloat16), "seq", -distance
        ).astype(jnp.float32)
    query_grad = (query_total * score_scale).astype(jnp.bfloat16)
    key_grad = pair_total[0].astype(jnp.bfloat16)
    value_grad = pair_total[1].astype(jnp.bfloat16)
    return (attended, query_grad, key_grad, value_grad)


def solution(mesh):
    in_specs = (
        P(("groups", "seq"), "heads", None),
        P(("groups", "seq"), "heads", None),
        P(("groups", "seq"), "heads", None),
        P(("groups", "seq"), "heads", None),
        P(None, ("groups", "seq")),
    )
    out_specs = (
        P(("groups", "seq"), "heads", None),
        P(("groups", "seq"), "heads", None),
        P(("groups", "seq"), "heads", None),
        P(("groups", "seq"), "heads", None),
    )
    return jax.shard_map(
        per_device, mesh=mesh, in_specs=in_specs, out_specs=out_specs, check_vma=False
    )
```

profile of v0, /device:TPU:0, one launch (start us, length us, event | category | flops | bytes accessed | tf_op | source)
XLA Modules:
  0.0 119.2 jit_solution(2337117231711554983)
XLA Ops:
  0.6 1.4 %copy_bitcast_fusion = (bf16[1,256,8,128]{3,1,2,0:T(8,128)(2,1)S(1)}, bf16[1,256,8,128]{3,1,2,0:T(8,128)(2,1)S(1)}) fusion(bf16[256,8,128]{2,1,0:T(8,128)(2,1)} %param.7, bf16[256,8,128]{2,1,0:T(8,128)(2,1)} %param.6), kind=kLoop, calls=%fused_computation.71 | loop fusion | bytes 2097152 | tf_op jit(solution)/shard_map/stack | solution.py:71
  2.1 1.1 pad_maximum_fusion
  3.2 5.9 %collective-permute-start = (bf16[2,256,8,128]{3,1,2,0:T(8,128)(2,1)}, bf16[2,256,8,128]{3,1,2,0:T(8,128)(2,1)}, u32[]{:S(2)}, u32[]{:S(2)}) collective-permute-start(bf16[2,256,8,128]{3,1,2,0:T(8,128)(2,1)} %pad_maximum_fusion), channel_id=1, source_target_pairs={{0,2},{2,4},{4,6},{6,8},{8,10},{10,12},{12,14},{1,3},{3,5},{5,7},{... | collective-permute-start | bytes 3145736 | tf_op jit(solution)/shard_map/ppermute | solution.py:18
  9.1 3.4 %collective-permute-start.1 = (bf16[2,256,8,128]{3,1,2,0:T(8,128)(2,1)}, bf16[2,256,8,128]{3,1,2,0:T(8,128)(2,1)}, u32[]{:S(2)}, u32[]{:S(2)}) collective-permute-start(bf16[2,256,8,128]{3,1,2,0:T(8,128)(2,1)} %pad_maximum_fusion), channel_id=1, source_target_pairs={{0,4},{2,6},{4,8},{6,10},{8,12},{10,14},{1,5},{3,7},{5,9},{7,11},{... | collective-permute-start | bytes 3145736 | tf_op jit(solution)/shard_map/ppermute | solution.py:18
  13.4 1.5 %fusion.54 = (f32[8,256]{1,0:T(8,128)S(1)}, f32[8,256,256]{1,2,0:T(8,128)S(1)}) fusion(bf16[256,8,128]{2,1,0:T(8,128)(2,1)S(1)} %copy-done.2, bf16[256,8,128]{2,1,0:T(8,128)(2,1)} %param.5, pred[256,256]{0,1:T(8,128)(4,1)S(1)} %get-tuple-element.17), kind=kOutput, calls=%fused_computation.94 | convolution fusion | flops 135788544 | bytes 3219456 | tf_op jit(solution)/shard_map/qhd,khd->hqk/dot_general | solution.py:33
  14.9 15.8 %collective-permute-done = bf16[2,256,8,128]{3,1,2,0:T(8,128)(2,1)} collective-permute-done((bf16[2,256,8,128]{3,1,2,0:T(8,128)(2,1)}, bf16[2,256,8,128]{3,1,2,0:T(8,128)(2,1)}, u32[]{:S(2)}, u32[]{:S(2)}) %collective-permute-start) | collective-permute-done | bytes 1048608 | tf_op jit(solution)/shard_map/ppermute | solution.py:18
  30.8 1.5 %fusion.55 = (f32[8,256]{1,0:T(8,128)S(1)}, f32[8,256,256]{1,2,0:T(8,128)S(1)}) fusion(bf16[256,8,128]{2,1,0:T(8,128)(2,1)S(1)} %copy-done.3, bf16[2,256,8,128]{3,1,2,0:T(8,128)(2,1)} %collective-permute-done, pred[256,256]{0,1:T(8,128)(4,1)S(1)} %get-tuple-element.15), kind=kOutput, calls=%fused_computation.95 | convolution fusion | flops 135788544 | bytes 3219456 | tf_op jit(solution)/shard_map/qhd,khd->hqk/dot_general | solution.py:33
  32.3 1.7 %collective-permute-done.1 = bf16[2,256,8,128]{3,1,2,0:T(8,128)(2,1)} collective-permute-done((bf16[2,256,8,128]{3,1,2,0:T(8,128)(2,1)}, bf16[2,256,8,128]{3,1,2,0:T(8,128)(2,1)}, u32[]{:S(2)}, u32[]{:S(2)}) %collective-permute-start.1) | collective-permute-done | bytes 1048608 | tf_op jit(solution)/shard_map/ppermute | solution.py:18
  34.0 1.5 %fusion.53 = (f32[8,256]{1,0:T(8,128)S(1)}, f32[8,256,256]{1,2,0:T(8,128)S(1)}) fusion(bf16[256,8,128]{2,1,0:T(8,128)(2,1)S(1)} %copy-done.3, bf16[2,256,8,128]{3,1,2,0:T(8,128)(2,1)} %collective-permute-done.1, pred[256,256]{0,1:T(8,128)(4,1)S(1)} %get-tuple-element.16), kind=kOutput, calls=%fused_computation.93 | convolution fusion | flops 135788544 | bytes 3219456 | tf_op jit(solution)/shard_map/qhd,khd->hqk/dot_general | solution.py:33
  35.5 0.5 convolution_bitcast_fusion
  36.0 1.0 fusion.6
  37.0 0.5 fusion.24
  37.9 1.6 %fusion.19 = f32[256,8,128]{0,2,1:T(8,128)S(1)} fusion(f32[256,8,128]{0,2,1:T(8,128)S(1)} %convolution_bitcast_fusion, f32[8,256,256]{1,2,0:T(8,128)S(1)} %get-tuple-element.26, f32[8,256]{1,0:T(8,128)S(1)} %maximum_maximum_fusion, bf16[2,256,8,128]{3,1,2,0:T(8,128)(2,1)} %collective-permute-done), kind=kOutput, calls=%fused_computation.42 | convolution fusion | flops 135528448 | bytes 4726784 | tf_op jit(solution)/shard_map/hqk,khd->qhd/dot_general | solution.py:41
  39.5 2.4 %multiply_reduce_fusion = (f32[256,8]{0,1:T(8,128)S(1)}, bf16[256,8,128]{0,2,1:T(8,128)(2,1)}) fusion(bf16[256,8,128]{0,2,1:T(8,128)(2,1)S(1)} %copy.24, f32[256,8]{0,1:T(8,128)S(1)} %get-tuple-element.14, f32[256,8,128]{0,2,1:T(8,128)S(1)} %fusion.19, f32[8,256,256]{1,2,0:T(8,128)S(1)} %get-tuple-element.22, f32[8,256]{1,0:T(8,128)S(1)} %maximum_maximum_fusion, ...), kind=kOutput, calls=%fused_computation.56 | convolution fusion | flops 137099264 | bytes 4743168 | tf_op jit(solution)/shard_map/hqk,khd->qhd/dot_general | solution.py:41
  41.9 0.5 multiply_convert_fusion
  42.4 1.9 %fusion.3 = bf16[8,256,256]{1,2,0:T(8,128)(2,1)S(1)} fusion(f32[8,256,256]{1,2,0:T(8,128)S(1)} %get-tuple-element.26, bf16[256,8,128]{0,2,1:T(8,128)(2,1)S(1)} %copy.24, f32[8,256]{1,0:T(8,128)S(1)} %bitcast.113, f32[8,256]{1,0:T(8,128)S(1)} %get-tuple-element.13, bf16[2,256,8,128]{3,1,2,0:T(8,128)(2,1)} %collective-permute-done), kind=kOutput, calls=%fused_computation.6 | convolution fusion | flops 136314880 | bytes 4210688 | tf_op jit(solution)/shard_map/qhd,khd->hqk/dot_general | solution.py:52
  44.8 1.1 pad_maximum_fusion.1
  45.9 1.3 %collective-permute-start.2 = (bf16[2,256,8,128]{3,1,2,0:T(8,128)(2,1)}, bf16[2,256,8,128]{3,1,2,0:T(8,128)(2,1)}, u32[]{:S(2)}, u32[]{:S(2)}) collective-permute-start(bf16[2,256,8,128]{3,1,2,0:T(8,128)(2,1)} %pad_maximum_fusion.1), channel_id=1, source_target_pairs={{2,0},{4,2},{6,4},{8,6},{10,8},{12,10},{14,12},{3,1},{5,3},{7,5},{... | collective-permute-start | bytes 3145736 | tf_op jit(solution)/shard_map/ppermute | solution.py:18
  47.2 1.6 %fusion.2 = bf16[8,256,256]{1,2,0:T(8,128)(2,1)S(1)} fusion(f32[8,256,256]{1,2,0:T(8,128)S(1)} %get-tuple-element.22, bf16[256,8,128]{0,2,1:T(8,128)(2,1)S(1)} %copy.24, f32[8,256]{1,0:T(8,128)S(1)} %bitcast.114, f32[8,256]{1,0:T(8,128)S(1)} %get-tuple-element.13, bf16[2,256,8,128]{3,1,2,0:T(8,128)(2,1)} %collective-permute-done.1), kind=kOutput, calls=%fused_computation.4 | convolution fusion | flops 136314880 | bytes 4210688 | tf_op jit(solution)/shard_map/qhd,khd->hqk/dot_general | solution.py:52
  49.2 1.1 pad_maximum_fusion.2
  50.3 1.5 %collective-permute-start.3 = (bf16[2,256,8,128]{3,1,2,0:T(8,128)(2,1)}, bf16[2,256,8,128]{3,1,2,0:T(8,128)(2,1)}, u32[]{:S(2)}, u32[]{:S(2)}) collective-permute-start(bf16[2,256,8,128]{3,1,2,0:T(8,128)(2,1)} %pad_maximum_fusion.2), channel_id=1, source_target_pairs={{4,0},{6,2},{8,4},{10,6},{12,8},{14,10},{5,1},{7,3},{9,5},{11,7},{... | collective-permute-start | bytes 3145736 | tf_op jit(solution)/shard_map/ppermute | solution.py:18
  51.8 0.5 convolution_bitcast_fusion.4
  52.3 1.5 %fusion.16 = f32[256,8,128]{2,0,1:T(8,128)S(1)} fusion(f32[256,8,128]{2,0,1:T(8,128)S(1)} %convolution_bitcast_fusion.4, bf16[8,256,256]{1,2,0:T(8,128)(2,1)S(1)} %fusion.3, bf16[2,256,8,128]{3,1,2,0:T(8,128)(2,1)} %collective-permute-done), kind=kOutput, calls=%fused_computation.36 | convolution fusion | flops 134479872 | bytes 3670016 | tf_op jit(solution)/shard_map/hqk,khd->qhd/dot_general | solution.py:54
  53.9 1.6 %fusion.23 = bf16[256,8,128]{2,0,1:T(8,128)(2,1)S(1)} fusion(f32[256,8,128]{2,0,1:T(8,128)S(1)} %fusion.16, bf16[8,256,256]{1,2,0:T(8,128)(2,1)S(1)} %fusion.2, bf16[2,256,8,128]{3,1,2,0:T(8,128)(2,1)} %collective-permute-done.1), kind=kOutput, calls=%fused_computation.48 | convolution fusion | flops 135004160 | bytes 3145728 | tf_op jit(solution)/shard_map/hqk,khd->qhd/dot_general | solution.py:54
  55.5 1.1 copy.43
  56.6 2.1 %copy.42 = bf16[256,8,128]{2,1,0:T(8,128)(2,1)} copy(bf16[256,8,128]{0,2,1:T(8,128)(2,1)} %get-tuple-element.28) | data formatting | bytes 1048576
  58.7 1.6 %fusion.13 = f32[1,256,8,128]{3,1,2,0:T(8,128)S(1)} fusion(bf16[8,256,256]{1,2,0:T(8,128)(2,1)} %copy-done, bf16[256,8,128]{2,1,0:T(8,128)(2,1)S(1)} %copy-done.4), kind=kOutput, calls=%fused_computation.29 | convolution fusion | flops 134479872 | bytes 2621440 | tf_op jit(solution)/shard_map/hqk,qhd->khd/dot_general | solution.py:58
  60.8 30.4 %collective-permute-done.2 = bf16[2,256,8,128]{3,1,2,0:T(8,128)(2,1)} collective-permute-done((bf16[2,256,8,128]{3,1,2,0:T(8,128)(2,1)}, bf16[2,256,8,128]{3,1,2,0:T(8,128)(2,1)}, u32[]{:S(2)}, u32[]{:S(2)}) %collective-permute-start.2) | collective-permute-done | bytes 1048608 | tf_op jit(solution)/shard_map/ppermute | solution.py:18
  91.2 23.6 %collective-permute-done.3 = bf16[2,256,8,128]{3,1,2,0:T(8,128)(2,1)} collective-permute-done((bf16[2,256,8,128]{3,1,2,0:T(8,128)(2,1)}, bf16[2,256,8,128]{3,1,2,0:T(8,128)(2,1)}, u32[]{:S(2)}, u32[]{:S(2)}) %collective-permute-start.3) | collective-permute-done | bytes 1048608 | tf_op jit(solution)/shard_map/ppermute | solution.py:18
  114.9 2.0 %fusion.1 = bf16[2,256,8,128]{3,1,2,0:T(8,128)(2,1)S(1)} fusion(f32[1,256,8,128]{3,1,2,0:T(8,128)S(1)} %convolution_bitcast_fusion.1, f32[1,256,8,128]{3,1,2,0:T(8,128)S(1)} %fusion.13, bf16[2,256,8,128]{3,1,2,0:T(8,128)(2,1)} %collective-permute-done.3, bf16[2,256,8,128]{3,1,2,0:T(8,128)(2,1)} %collective-permute-done.2), kind=kLoop, calls=%fused_computation.2 | loop fusion | flops 3145728 | bytes 5242880 | tf_op jit(solution)/shard_map/convert.1
  116.9 1.1 copy.44
  118.1 1.1 copy.45
  (27 shorter events, 2.6 us)
Async XLA Ops:
  0.6 11.9 %copy-start.5 = (bf16[256,8,128]{2,1,0:T(8,128)(2,1)S(1)}, bf16[256,8,128]{2,1,0:T(8,128)(2,1)}, u32[]{:S(2)}) copy-start(bf16[256,8,128]{2,1,0:T(8,128)(2,1)} %param.8) | copy-start | bytes 1572868
  2.1 10.8 %copy-start.6 = (s32[3,256]{1,0:T(4,128)S(1)}, s32[3,256]{1,0:T(4,128)}, u32[]{:S(2)}) copy-start(s32[3,256]{1,0:T(4,128)} %param.9) | copy-start | bytes 9220
  2.1 11.2 %copy-start.2 = (bf16[256,8,128]{2,1,0:T(8,128)(2,1)S(1)}, bf16[256,8,128]{2,1,0:T(8,128)(2,1)}, u32[]{:S(2)}) copy-start(bf16[256,8,128]{2,1,0:T(8,128)(2,1)} %param.6) | copy-start | bytes 1572868
  3.2 27.6 %collective-permute-start = (bf16[2,256,8,128]{3,1,2,0:T(8,128)(2,1)}, bf16[2,256,8,128]{3,1,2,0:T(8,128)(2,1)}, u32[]{:S(2)}, u32[]{:S(2)}) collective-permute-start(bf16[2,256,8,128]{3,1,2,0:T(8,128)(2,1)} %pad_maximum_fusion), channel_id=1, source_target_pairs={{0,2},{2,4},{4,6},{6,8},{8,10},{10,12},{12,14},{1,3},{3,5},{5,7},{... | collective-permute-start | bytes 3145736 | tf_op jit(solution)/shard_map/ppermute | solution.py:18
  9.1 24.9 %collective-permute-start.1 = (bf16[2,256,8,128]{3,1,2,0:T(8,128)(2,1)}, bf16[2,256,8,128]{3,1,2,0:T(8,128)(2,1)}, u32[]{:S(2)}, u32[]{:S(2)}) collective-permute-start(bf16[2,256,8,128]{3,1,2,0:T(8,128)(2,1)} %pad_maximum_fusion), channel_id=1, source_target_pairs={{0,4},{2,6},{4,8},{6,10},{8,12},{10,14},{1,5},{3,7},{5,9},{7,11},{... | collective-permute-start | bytes 3145736 | tf_op jit(solution)/shard_map/ppermute | solution.py:18
  12.8 17.9 %copy-start.3 = (bf16[256,8,128]{2,1,0:T(8,128)(2,1)S(1)}, bf16[256,8,128]{2,1,0:T(8,128)(2,1)}, u32[]{:S(2)}) copy-start(bf16[256,8,128]{2,1,0:T(8,128)(2,1)} %param.5) | copy-start | bytes 1572868
  32.3 3.2 %copy-start.1 = (bf16[256,8,128]{2,1,0:T(8,128)(2,1)S(1)}, bf16[256,8,128]{2,1,0:T(8,128)(2,1)}, u32[]{:S(2)}) copy-start(bf16[256,8,128]{2,1,0:T(8,128)(2,1)} %param.7) | copy-start | bytes 1572868
  42.4 9.3 %copy-start = (bf16[8,256,256]{1,2,0:T(8,128)(2,1)}, bf16[8,256,256]{1,2,0:T(8,128)(2,1)S(1)}, u32[]{:S(2)}) copy-start(bf16[8,256,256]{1,2,0:T(8,128)(2,1)S(1)} %multiply_convert_fusion) | copy-start | bytes 3145732
  45.9 45.3 %collective-permute-start.2 = (bf16[2,256,8,128]{3,1,2,0:T(8,128)(2,1)}, bf16[2,256,8,128]{3,1,2,0:T(8,128)(2,1)}, u32[]{:S(2)}, u32[]{:S(2)}) collective-permute-start(bf16[2,256,8,128]{3,1,2,0:T(8,128)(2,1)} %pad_maximum_fusion.1), channel_id=1, source_target_pairs={{2,0},{4,2},{6,4},{8,6},{10,8},{12,10},{14,12},{3,1},{5,3},{7,5},{... | collective-permute-start | bytes 3145736 | tf_op jit(solution)/shard_map/ppermute | solution.py:18
  50.3 64.6 %collective-permute-start.3 = (bf16[2,256,8,128]{3,1,2,0:T(8,128)(2,1)}, bf16[2,256,8,128]{3,1,2,0:T(8,128)(2,1)}, u32[]{:S(2)}, u32[]{:S(2)}) collective-permute-start(bf16[2,256,8,128]{3,1,2,0:T(8,128)(2,1)} %pad_maximum_fusion.2), channel_id=1, source_target_pairs={{4,0},{6,2},{8,4},{10,6},{12,8},{14,10},{5,1},{7,3},{9,5},{11,7},{... | collective-permute-start | bytes 3145736 | tf_op jit(solution)/shard_map/ppermute | solution.py:18
  53.8 4.9 %copy-start.4 = (bf16[256,8,128]{2,1,0:T(8,128)(2,1)S(1)}, bf16[256,8,128]{2,1,0:T(8,128)(2,1)}, u32[]{:S(2)}) copy-start(bf16[256,8,128]{2,1,0:T(8,128)(2,1)} %param.5) | copy-start | bytes 1572868
where the time goes:
time: 120 us; the launch traced here: 119 us
  waiting for transfers between devices  71.6 us (60%)
  matrix products  20.6 us (17%)
  starting transfers between devices  12.1 us (10%)
  local copies, waits for them, and re-layouts  7.42 us (6%)
  other arithmetic  6.66 us (6%)
    ppermute x4, waiting for transfers between devices, from_behind(): return lax.ppermute(value, axis, pairs)  71.6 us
    ppermute x4, starting transfers between devices, from_behind(): return lax.ppermute(value, axis, pairs)  12.1 us
    unnamed x19, local copies, waits for them, and re-layouts  5.89 us
    dot_general x3, matrix products, masked_scores(): jnp.einsum('qhd,khd->hqk', queries, kv_tile[0], preferred_element_type=jn...  4.57 us
    dot_general x3, matrix products, forward_part(): jnp.einsum('hqk,khd->qhd', weights.astype(jnp.bfloat16), kv_tile[1], pref...  4.48 us
    dot_general x3, matrix products, backward_part(): jnp.einsum('qhd,khd->hqk', out_grad, kv_tile[1], preferred_element_type=j...  4.03 us
    dot_general x3, matrix products, backward_part(): jnp.einsum('hqk,khd->qhd', score_grad, kv_tile[0], preferred_element_type...  3.64 us
    dot_general x3, matrix products, backward_part(): jnp.einsum('hqk,qhd->khd', score_grad, queries, preferred_element_type=jn...  2.49 us
  transfers between devices with their start and end apart: 4, of which 4 were waited for; matrix products, arithmetic and copies ran while one was open for 13% of the time, Pallas kernels for 0%

commit v1 on v0

v1 whole, which is shorter than its diff:
```python
import functools
import math

import jax
import jax.numpy as jnp
from jax import lax
from jax.experimental import pallas as pl
from jax.experimental.pallas import tpu as pltpu
from jax.sharding import PartitionSpec as P

NEG = -1e30
MESH = pl.DeviceIdType.MESH
F32 = jnp.float32
BF16 = jnp.bfloat16


def dot_nt(a, b):
    return lax.dot_general(a, b, (((1,), (1,)), ((), ())), preferred_element_type=F32)


def dot_tn(a, b):
    return lax.dot_general(a, b, (((0,), (0,)), ((), ())), preferred_element_type=F32)


def dot_nn(a, b):
    return lax.dot_general(a, b, (((1,), (0,)), ((), ())), preferred_element_type=F32)


def kernel(
    count, tok, half, head_size,
    arg_ref, spans_ref, out_ref,
    kv, qd, span_own, span_other, bias, s_buf, dp_buf, grads, halo_out, halo_back, od, last,
    span_sem, kv_sem, qd_sem, own_sem, fwd_sem, back_sem, od_sem, last_sem,
):
    me = lax.axis_index("seq")
    x = lax.rem(me, 2)
    other = 1 - x
    pair = lax.div(me, 2)
    partner = me + 1 - 2 * x
    has_next = me + 2 < count
    has_prev = me >= 2
    score_scale = 1.0 / math.sqrt(head_size)

    def remote(src, dst, sems, at, to):
        return pltpu.make_async_remote_copy(
            src_ref=src,
            dst_ref=dst,
            send_sem=sems.at[(0,) + at],
            recv_sem=sems.at[(1,) + at],
            device_id={"seq": to},
            device_id_type=MESH,
        )

    def send_spans():
        return remote(span_own, span_other, span_sem, (), partner)

    def send_kv(i):
        src = arg_ref.at[other * half + i, pl.ds(0, 2)]
        return remote(src, kv.at[i, :, 2 + x], kv_sem, (i,), partner)

    def send_qd(i):
        src = arg_ref.at[other * half + i, pl.ds(2, 2)]
        return remote(src, qd.at[i, x], qd_sem, (i,), partner)

    def send_own(i):
        src = arg_ref.at[x * half + i, pl.ds(0, 2)]
        return remote(src, kv.at[i, :, x], own_sem, (i,), me + 2)

    def send_fwd(i):
        return remote(kv.at[i, :, 2 + other], kv.at[i, :, other], fwd_sem, (i,), me + 2)

    def send_back(i, block):
        return remote(halo_out.at[i, block], halo_back.at[i, block], back_sem, (i, block), me - 2)

    def send_od(i):
        dst = out_ref.at[x * half + i, pl.ds(0, 2)]
        return remote(od.at[i, other], dst, od_sem, (i,), partner)

    def send_last(i):
        dst = out_ref.at[x * half + i, pl.ds(2, 2)]
        return remote(last.at[i], dst, last_sem, (i,), partner)

    def land_kv(i):
        dst = kv.at[i, :, 2 + other]
        return remote(arg_ref.at[0, pl.ds(0, 2)], dst, kv_sem, (i,), partner)

    def land_qd(i):
        return remote(arg_ref.at[0, pl.ds(2, 2)], qd.at[i, other], qd_sem, (i,), partner)

    def land_own(i):
        return remote(arg_ref.at[0, pl.ds(0, 2)], kv.at[i, :, x], own_sem, (i,), partner)

    def land_fwd(i):
        return remote(arg_ref.at[0, pl.ds(0, 2)], kv.at[i, :, other], fwd_sem, (i,), partner)

    def land_back(i, block):
        return send_back(i, block)

    def land_od(i):
        dst = out_ref.at[other * half + i, pl.ds(0, 2)]
        return remote(last.at[i], dst, od_sem, (i,), partner)

    def land_last(i):
        dst = out_ref.at[other * half + i, pl.ds(2, 2)]
        return remote(last.at[i], dst, last_sem, (i,), partner)

    barrier = pltpu.get_barrier_semaphore()
    pl.semaphore_signal(barrier, inc=1, device_id={"seq": partner}, device_id_type=MESH)

    @pl.when(has_next)
    def _():
        pl.semaphore_signal(barrier, inc=1, device_id={"seq": me + 2}, device_id_type=MESH)

    @pl.when(has_prev)
    def _():
        pl.semaphore_signal(barrier, inc=1, device_id={"seq": me - 2}, device_id_type=MESH)

    span_own[...] = jnp.zeros_like(span_own)
    span_own[0:3, :] = spans_ref[...]
    pl.semaphore_wait(barrier, 1 + has_next.astype(jnp.int32) + has_prev.astype(jnp.int32))

    send_spans().start()
    for i in range(half):
        send_kv(i).start()
        send_qd(i).start()

    @pl.when(has_next)
    def _():
        for i in range(half):
            send_own(i).start()

    @pl.when(jnp.logical_not(has_prev))
    def _():
        for i in range(half):
            for which in range(2):
                kv[i, which, 0:2] = jnp.zeros((2, tok, head_size), BF16)

    @pl.when(jnp.logical_not(has_next))
    def _():
        halo_back[...] = jnp.zeros_like(halo_back)

    for i in range(half):
        kv[i, :, 2 + x] = arg_ref[x * half + i, 0:2]
        qd[i, x] = arg_ref[x * half + i, 2:4]

    send_spans().wait_recv()
    lane = lax.broadcasted_iota(jnp.int32, (1, tok), 1)
    for block in range(2):
        mine = x == block
        start_at = pair * (2 * tok) + block * tok
        low, chosen, rejected = [
            jnp.where(mine, span_own[r : r + 1, :], span_other[r : r + 1, :]) - start_at
            for r in range(3)
        ]
        chosen = jnp.where(lane >= rejected, chosen, 2 * tok)
        for part in range(3):
            at = lax.broadcasted_iota(jnp.int32, (tok, tok), 0) + (part - 2) * tok
            seen = (at >= low) & (at <= lane) & ((at < chosen) | (at >= rejected))
            bias[block, part] = jnp.where(seen, 0.0, NEG)

    def compute(i):
        for block in range(2):
            queries = qd[i, block, 0]
            out_grad = qd[i, block, 1]
            row_max = jnp.full((1, tok), -jnp.inf, F32)
            for part in range(3):
                raw = dot_nt(kv[i, 0, block + part], queries)
                scores = raw * (score_scale * math.log2(math.e)) + bias[block, part]
                s_buf[part] = scores
                row_max = jnp.maximum(row_max, jnp.max(scores, axis=0, keepdims=True))
            row_sum = jnp.zeros((1, tok), F32)
            delta = jnp.zeros((1, tok), F32)
            mixed = jnp.zeros((head_size, tok), F32)
            for part in range(3):
                weights = jnp.exp2(s_buf[part] - row_max)
                row_sum = row_sum + jnp.sum(weights, axis=0, keepdims=True)
                values = kv[i, 1, block + part]
                prob_grad = dot_nt(values, out_grad)
                delta = delta + jnp.sum(weights * prob_grad, axis=0, keepdims=True)
                s_buf[part] = weights
                dp_buf[part] = prob_grad
                mixed = mixed + dot_tn(values, weights.astype(BF16))
            inverse = 1.0 / row_sum
            delta = delta * inverse
            od[i, block, 0] = (mixed * inverse).T.astype(BF16)
            query_grad = jnp.zeros((head_size, tok), F32)
            for part in range(3):
                probs = s_buf[part] * inverse
                score_grad = (probs * (dp_buf[part] - delta)).astype(BF16)
                value_part = dot_nn(probs.astype(BF16), out_grad)
                key_part = dot_nn(score_grad, queries) * score_scale
                query_grad = query_grad + dot_tn(kv[i, 0, block + part], score_grad)
                at = block + part
                if block == 1 and part < 2:
                    key_part = key_part + grads[i, at, 0]
                    value_part = value_part + grads[i, at, 1]
                grads[i, at, 0] = key_part
                grads[i, at, 1] = value_part
            od[i, block, 1] = (query_grad * score_scale).T.astype(BF16)

    def finish(i):
        @pl.when(has_next)
        def _():
            land_back(i, other).wait_recv()

        last[i] = (grads[i, 2 + other] + halo_back[i, other].astype(F32)).astype(BF16)
        send_last(i).start()

        @pl.when(has_next)
        def _():
            land_back(i, x).wait_recv()

        done = grads[i, 2 + x] + halo_back[i, x].astype(F32)
        out_ref[x * half + i, 2:4] = done.astype(BF16)

    def step(i, carry):
        land_kv(i).wait_recv()

        @pl.when(has_next)
        def _():
            send_fwd(i).start()

        land_qd(i).wait_recv()

        @pl.when(has_prev)
        def _():
            land_own(i).wait_recv()
            land_fwd(i).wait_recv()

        compute(i)

        @pl.when(has_prev)
        def _():
            halo_out[i] = grads[i, 0:2].astype(BF16)
            send_back(i, other).start()
            send_back(i, x).start()

        send_od(i).start()
        out_ref[x * half + i, 0:2] = od[i, x]

        @pl.when(i > 0)
        def _():
            finish(i - 1)

        return carry

    lax.fori_loop(0, half, step, 0)
    finish(half - 1)

    send_spans().wait_send()
    for i in range(half):
        send_kv(i).wait_send()
        send_qd(i).wait_send()
        send_od(i).wait_send()
        send_last(i).wait_send()
        land_od(i).wait_recv()
        land_last(i).wait_recv()

    @pl.when(has_next)
    def _():
        for i in range(half):
            send_own(i).wait_send()
            send_fwd(i).wait_send()

    @pl.when(has_prev)
    def _():
        for i in range(half):
            send_back(i, other).wait_send()
            send_back(i, x).wait_send()


def per_device(count, queries, keys, values, out_grad, spans):
    tok, heads, head_size = queries.shape
    half = heads // 2
    packed = jnp.stack([a.transpose(1, 0, 2) for a in (keys, values, queries, out_grad)], axis=1)
    vmem = pltpu.VMEM
    dma = pltpu.SemaphoreType.DMA
    blocks = 3 * 2 * heads // 2
    out = pl.pallas_call(
        functools.partial(kernel, count, tok, half, head_size),
        out_shape=jax.ShapeDtypeStruct((heads, 4, tok, head_size), BF16),
        in_specs=[pl.BlockSpec(memory_space=vmem)] * 2,
        out_specs=pl.BlockSpec(memory_space=vmem),
        scratch_shapes=[
            vmem((half, 2, 4, tok, head_size), BF16),
            vmem((half, 2, 2, tok, head_size), BF16),
            vmem((8, tok), jnp.int32),
            vmem((8, tok), jnp.int32),
            vmem((2, 3, tok, tok), F32),
            vmem((3, tok, tok), F32),
            vmem((3, tok, tok), F32),
            vmem((half, 4, 2, tok, head_size), F32),
            vmem((half, 2, 2, tok, head_size), BF16),
            vmem((half, 2, 2, tok, head_size), BF16),
            vmem((half, 2, 2, tok, head_size), BF16),
            vmem((half, 2, tok, head_size), BF16),
            dma((2,)),
            dma((2, half)),
            dma((2, half)),
            dma((2, half)),
            dma((2, half)),
            dma((2, half, 2)),
            dma((2, half)),
            dma((2, half)),
        ],
        compiler_params=pltpu.CompilerParams(
            collective_id=0, has_side_effects=True, vmem_limit_bytes=48 * 1024 * 1024
        ),
        cost_estimate=pl.CostEstimate(
            flops=blocks * 12 * tok * tok * head_size,
            bytes_accessed=16 * heads * tok * head_size,
            transcendentals=blocks * tok * tok,
        ),
    )(packed, spans)
    return tuple(out[:, r].transpose(1, 0, 2) for r in range(4))


def solution(mesh):
    spec = P(("groups", "seq"), "heads", None)
    return jax.shard_map(
        functools.partial(per_device, mesh.shape["seq"]),
        mesh=mesh,
        in_specs=(spec,) * 4 + (P(None, ("groups", "seq")),),
        out_specs=(spec,) * 4,
        check_vma=False,
    )
```

time: 120 us -> 58.6 us (0.49)
  waiting for transfers between devices: 71.6 us -> 0 us
  Pallas kernels: 0 us -> 50.6 us
  matrix products: 20.6 us -> 0 us
  starting transfers between devices: 12.1 us -> 0 us
  other arithmetic: 6.66 us -> 0.26 us
    ppermute x4 -> x0, waiting for transfers between devices: 71.6 us -> none  [from_behind(): return lax.ppermute(value, axis, pairs)]
    pallas_call x0 -> x1, Pallas kernels: none -> 50.6 us  [per_device(): pl.pallas_call(functools.partial(kernel, count, tok, half, head_size), ou...]
    dot_general x18 -> x0, matrix products: 20.6 us -> none  [the longest x3 4.57 us: masked_scores(): jnp.einsum('qhd,khd->hqk', queries, kv_tile[0], preferred_element_type=jn...]
    ppermute x4 -> x0, starting transfers between devices: 12.1 us -> none  [from_behind(): return lax.ppermute(value, axis, pairs)]
    another operation x4 -> x1, other arithmetic: 5.23 us -> 0.26 us  [per_device(): jnp.stack([a.transpose(1, 0, 2) for a in (keys, values, queries, out_grad...]
    unnamed x19 -> x10, local copies, waits for them, and re-layouts: 5.89 us -> 4.96 us
  transfers between devices with their start and end apart: 4 -> 0, of which waited for: 4 -> 0; matrix products, arithmetic and copies ran while one was open for 13% -> 0% of each run, Pallas kernels for 0% -> 0%
where the time goes in v1:
time: 58.6 us; the launch traced here: 58.4 us
  Pallas kernels  50.6 us (86%)
  local copies, waits for them, and re-layouts  6.76 us (12%)
  between operations  0.71 us (1%)
    pallas_call x1, Pallas kernels, per_device(): pl.pallas_call(functools.partial(kernel, count, tok, half, head_size), ou...  50.6 us
    unnamed x10, local copies, waits for them, and re-layouts  4.96 us
    another operation x2, local copies, waits for them, and re-layouts, per_device(): jnp.stack([a.transpose(1, 0, 2) for a in (keys, values, queries, out_grad...  1.66 us

profile of v1, /device:TPU:0, one launch (start us, length us, event | category | flops | bytes accessed | tf_op | source)
XLA Modules:
  0.0 58.4 jit_solution(3441672207881588592)
XLA Ops:
  0.6 0.0 copy-start.1
  0.6 0.0 copy-start.2
  0.7 1.5 %copy_bitcast_fusion = (bf16[8,1,256,128]{3,2,1,0:T(8,128)(2,1)S(1)}, bf16[8,1,256,128]{3,2,1,0:T(8,128)(2,1)S(1)}) fusion(bf16[256,8,128]{2,1,0:T(8,128)(2,1)} %param.8, bf16[256,8,128]{2,1,0:T(8,128)(2,1)} %param.5), kind=kLoop, calls=%fused_computation.1 | loop fusion | bytes 2097152 | tf_op jit(solution)/shard_map/stack | solution.py:275
  2.1 0.0 copy-done.1
  2.1 0.0 copy-done.2
  2.2 0.2 copy_bitcast_fusion.2
  2.3 0.0 copy-start
  2.4 0.3 pad_maximum_fusion.arg_ref
  2.6 0.4 copy-done
  3.0 50.6 %shard_map.84 = bf16[8,4,256,128]{3,2,1,0:T(8,128)(2,1)S(1)} custom-call(bf16[8,4,256,128]{3,2,1,0:T(8,128)(2,1)S(1)} %pad_maximum_fusion.arg_ref, s32[3,256]{1,0:T(4,128)S(1)} %copy-done), custom_call_target="tpu_custom_call" | custom-call | flops 2415919104 | bytes 4194304 | tf_op jit(solution)/shard_map/pallas_call | solution.py:279
  53.7 0.1 slice_bitcast_fusion
  53.8 1.1 %copy.16 = bf16[256,8,128]{2,1,0:T(8,128)(2,1)} copy(bf16[256,8,128]{2,0,1:T(8,128)(2,1)S(1)} %get-tuple-element.8) | data formatting | bytes 1048576
  55.0 1.1 %copy.15 = bf16[256,8,128]{2,1,0:T(8,128)(2,1)} copy(bf16[256,8,128]{2,0,1:T(8,128)(2,1)S(1)} %get-tuple-element.9) | data formatting | bytes 1048576
  56.1 1.1 %copy.14 = bf16[256,8,128]{2,1,0:T(8,128)(2,1)} copy(bf16[256,8,128]{2,0,1:T(8,128)(2,1)S(1)} %get-tuple-element.10) | data formatting | bytes 1048576
  57.2 1.1 %copy.13 = bf16[256,8,128]{2,1,0:T(8,128)(2,1)} copy(bf16[256,8,128]{2,0,1:T(8,128)(2,1)S(1)} %get-tuple-element.11) | data formatting | bytes 1048576
Async XLA Ops:
  0.6 1.5 %copy-start.1 = (bf16[256,8,128]{2,1,0:T(8,128)(2,1)S(1)}, bf16[256,8,128]{2,1,0:T(8,128)(2,1)}, u32[]{:S(2)}) copy-start(bf16[256,8,128]{2,1,0:T(8,128)(2,1)} %param.7) | copy-start | bytes 1572868
  0.6 1.5 %copy-start.2 = (bf16[256,8,128]{2,1,0:T(8,128)(2,1)S(1)}, bf16[256,8,128]{2,1,0:T(8,128)(2,1)}, u32[]{:S(2)}) copy-start(bf16[256,8,128]{2,1,0:T(8,128)(2,1)} %param.6) | copy-start | bytes 1572868
  2.3 0.7 %copy-start = (s32[3,256]{1,0:T(4,128)S(1)}, s32[3,256]{1,0:T(4,128)}, u32[]{:S(2)}) copy-start(s32[3,256]{1,0:T(4,128)} %spans_ref.1) | copy-start | bytes 9220

commit v2 on v1

--- a/solution.py
+++ b/solution.py
@@ -28,8 +28,9 @@
 
 def kernel(
     count, tok, half, head_size,
-    arg_ref, spans_ref, out_ref,
-    kv, qd, span_own, span_other, bias, s_buf, dp_buf, grads, halo_out, halo_back, od, last,
+    key_ref, value_ref, query_ref, grad_ref, spans_ref,
+    att_out, query_out, key_out, value_out,
+    arg_ref, stage, od_in, last_in, kv, qd, span_own, span_other, bias, s_buf, dp_buf, grads, halo_out, halo_back, od, last,
     span_sem, kv_sem, qd_sem, own_sem, fwd_sem, back_sem, od_sem, last_sem,
 ):
     me = lax.axis_index("seq")
@@ -73,12 +74,10 @@
         return remote(halo_out.at[i, block], halo_back.at[i, block], back_sem, (i, block), me - 2)
 
     def send_od(i):
-        dst = out_ref.at[x * half + i, pl.ds(0, 2)]
-        return remote(od.at[i, other], dst, od_sem, (i,), partner)
+        return remote(od.at[i, other], od_in.at[i], od_sem, (i,), partner)
 
     def send_last(i):
-        dst = out_ref.at[x * half + i, pl.ds(2, 2)]
-        return remote(last.at[i], dst, last_sem, (i,), partner)
+        return remote(last.at[i], last_in.at[i], last_sem, (i,), partner)
 
     def land_kv(i):
         dst = kv.at[i, :, 2 + other]
@@ -96,13 +95,21 @@
     def land_back(i, block):
         return send_back(i, block)
 
-    def land_od(i):
-        dst = out_ref.at[other * half + i, pl.ds(0, 2)]
-        return remote(last.at[i], dst, od_sem, (i,), partner)
-
-    def land_last(i):
-        dst = out_ref.at[other * half + i, pl.ds(2, 2)]
-        return remote(last.at[i], dst, last_sem, (i,), partner)
+    rows = 2 * half * tok
+
+    def head_rows(which, head):
+        return pl.ds(which * rows + head, tok, stride=2 * half)
+
+    def pack(which, ref):
+        stage[which * rows : (which + 1) * rows, :] = ref[...].astype(F32)
+        for head in range(2 * half):
+            arg_ref[head, which] = stage[head_rows(which, head), :].astype(BF16)
+
+    def unpack(which, head, block):
+        stage[head_rows(which, head), :] = block.astype(F32)
+
+    def write(which, ref):
+        ref[...] = stage[which * rows : (which + 1) * rows, :].astype(BF16)
 
     barrier = pltpu.get_barrier_semaphore()
     pl.semaphore_signal(barrier, inc=1, device_id={"seq": partner}, device_id_type=MESH)
@@ -117,17 +124,23 @@
 
     span_own[...] = jnp.zeros_like(span_own)
     span_own[0:3, :] = spans_ref[...]
+    pack(0, key_ref)
+    pack(1, value_ref)
     pl.semaphore_wait(barrier, 1 + has_next.astype(jnp.int32) + has_prev.astype(jnp.int32))
 
     send_spans().start()
     for i in range(half):
         send_kv(i).start()
-        send_qd(i).start()
 
     @pl.when(has_next)
     def _():
         for i in range(half):
             send_own(i).start()
+
+    pack(2, query_ref)
+    pack(3, grad_ref)
+    for i in range(half):
+        send_qd(i).start()
 
     @pl.when(jnp.logical_not(has_prev))
     def _():
@@ -211,7 +224,8 @@
             land_back(i, x).wait_recv()
 
         done = grads[i, 2 + x] + halo_back[i, x].astype(F32)
-        out_ref[x * half + i, 2:4] = done.astype(BF16)
+        for which in range(2):
+            unpack(2 + which, x * half + i, done[which])
 
     def step(i, carry):
         land_kv(i).wait_recv()
@@ -236,7 +250,8 @@
             send_back(i, x).start()
 
         send_od(i).start()
-        out_ref[x * half + i, 0:2] = od[i, x]
+        for which in range(2):
+            unpack(which, x * half + i, od[i, x, which])
 
         @pl.when(i > 0)
         def _():
@@ -246,6 +261,19 @@
 
     lax.fori_loop(0, half, step, 0)
     finish(half - 1)
+
+    for i in range(half):
+        send_od(i).wait_recv()
+        for which in range(2):
+            unpack(which, other * half + i, od_in[i, which])
+        if i == half - 1:
+            write(0, att_out)
+            write(1, query_out)
+        send_last(i).wait_recv()
+        for which in range(2):
+            unpack(2 + which, other * half + i, last_in[i, which])
+    write(2, key_out)
+    write(3, value_out)
 
     send_spans().wait_send()
     for i in range(half):
@@ -253,8 +281,6 @@
         send_qd(i).wait_send()
         send_od(i).wait_send()
         send_last(i).wait_send()
-        land_od(i).wait_recv()
-        land_last(i).wait_recv()
 
     @pl.when(has_next)
     def _():
@@ -272,16 +298,20 @@
 def per_device(count, queries, keys, values, out_grad, spans):
     tok, heads, head_size = queries.shape
     half = heads // 2
-    packed = jnp.stack([a.transpose(1, 0, 2) for a in (keys, values, queries, out_grad)], axis=1)
+    flat = [a.reshape(tok * heads, head_size) for a in (keys, values, queries, out_grad)]
     vmem = pltpu.VMEM
     dma = pltpu.SemaphoreType.DMA
     blocks = 3 * 2 * heads // 2
     out = pl.pallas_call(
         functools.partial(kernel, count, tok, half, head_size),
-        out_shape=jax.ShapeDtypeStruct((heads, 4, tok, head_size), BF16),
-        in_specs=[pl.BlockSpec(memory_space=vmem)] * 2,
-        out_specs=pl.BlockSpec(memory_space=vmem),
+        out_shape=[jax.ShapeDtypeStruct((tok * heads, head_size), BF16)] * 4,
+        in_specs=[pl.BlockSpec(memory_space=vmem)] * 5,
+        out_specs=[pl.BlockSpec(memory_space=vmem)] * 4,
         scratch_shapes=[
+            vmem((heads, 4, tok, head_size), BF16),
+            vmem((4 * heads * tok, head_size), F32),
+            vmem((half, 2, tok, head_size), BF16),
+            vmem((half, 2, tok, head_size), BF16),
             vmem((half, 2, 4, tok, head_size), BF16),
             vmem((half, 2, 2, tok, head_size), BF16),
             vmem((8, tok), jnp.int32),
@@ -311,8 +341,8 @@
             bytes_accessed=16 * heads * tok * head_size,
             transcendentals=blocks * tok * tok,
         ),
-    )(packed, spans)
-    return tuple(out[:, r].transpose(1, 0, 2) for r in range(4))
+    )(*flat, spans)
+    return tuple(a.reshape(tok, heads, head_size) for a in out)
 
 
 def solution(mesh):

time: 58.6 us -> 60 us (1.024)
  local copies, waits for them, and re-layouts: 6.76 us -> 8.02 us
    unnamed x10 -> x14, local copies, waits for them, and re-layouts: 4.96 us -> 8.02 us
    another operation x2 -> x0, local copies, waits for them, and re-layouts: 1.66 us -> none  [per_device(): jnp.stack([a.transpose(1, 0, 2) for a in (keys, values, queries, out_grad...]
where the time goes in v2:
time: 60 us; the launch traced here: 59.6 us
  Pallas kernels  51 us (85%)
  local copies, waits for them, and re-layouts  8.02 us (13%)
  between operations  0.65 us (1%)
    pallas_call x1, Pallas kernels, per_device(): pl.pallas_call(functools.partial(kernel, count, tok, half, head_size), ou...  51 us
    unnamed x14, local copies, waits for them, and re-layouts  8.02 us

profile of v2, /device:TPU:0, one launch (start us, length us, event | category | flops | bytes accessed | tf_op | source)
XLA Modules:
  0.0 59.6 jit_solution(9840195523043440149)
XLA Ops:
  0.6 0.0 copy-start.4
  0.6 0.7 %copy-done.4 = s32[3,256]{1,0:T(4,128)S(1)} copy-done((s32[3,256]{1,0:T(4,128)S(1)}, s32[3,256]{1,0:T(4,128)}, u32[]{:S(2)}) %copy-start.4) | copy-done | bytes 3096
  1.3 0.0 copy-start
  1.3 1.0 %copy-done = bf16[256,8,128]{2,1,0:T(8,128)(2,1)S(1)} copy-done((bf16[256,8,128]{2,1,0:T(8,128)(2,1)S(1)}, bf16[256,8,128]{2,1,0:T(8,128)(2,1)}, u32[]{:S(2)}) %copy-start) | copy-done | bytes 524312
  2.4 0.0 copy-start.1
  2.4 1.0 %copy-done.1 = bf16[256,8,128]{2,1,0:T(8,128)(2,1)S(1)} copy-done((bf16[256,8,128]{2,1,0:T(8,128)(2,1)S(1)}, bf16[256,8,128]{2,1,0:T(8,128)(2,1)}, u32[]{:S(2)}) %copy-start.1) | copy-done | bytes 524312
  3.4 0.0 copy-start.2
  3.4 1.0 %copy-done.2 = bf16[256,8,128]{2,1,0:T(8,128)(2,1)S(1)} copy-done((bf16[256,8,128]{2,1,0:T(8,128)(2,1)S(1)}, bf16[256,8,128]{2,1,0:T(8,128)(2,1)}, u32[]{:S(2)}) %copy-start.2) | copy-done | bytes 524312
  4.4 0.0 copy-start.3
  4.4 1.0 %copy-done.3 = bf16[256,8,128]{2,1,0:T(8,128)(2,1)S(1)} copy-done((bf16[256,8,128]{2,1,0:T(8,128)(2,1)S(1)}, bf16[256,8,128]{2,1,0:T(8,128)(2,1)}, u32[]{:S(2)}) %copy-start.3) | copy-done | bytes 524312
  5.5 51.0 %shard_map.84 = (bf16[2048,128]{1,0:T(8,128)(2,1)S(1)}, bf16[2048,128]{1,0:T(8,128)(2,1)S(1)}, bf16[2048,128]{1,0:T(8,128)(2,1)S(1)}, bf16[2048,128]{1,0:T(8,128)(2,1)S(1)}) custom-call(bf16[2048,128]{1,0:T(8,128)(2,1)S(1)} %bitcast.12, bf16[2048,128]{1,0:T(8,128)(2,1)S(1)} %bitcast.13, bf16[2048,128]{1,0:T(8,128)(2,1)S(1)} %bitcast.14, ...), custom_call_target="tpu_custom_call" | custom-call | flops 2415919104 | bytes 4194304 | tf_op jit(solution)/shard_map/pallas_call | solution.py:305
  56.4 0.8 %copy.13 = bf16[256,8,128]{2,1,0:T(8,128)(2,1)} copy(bf16[256,8,128]{2,1,0:T(8,128)(2,1)S(1)} %bitcast.11) | data formatting | bytes 1048576
  57.2 0.8 %copy.14 = bf16[256,8,128]{2,1,0:T(8,128)(2,1)} copy(bf16[256,8,128]{2,1,0:T(8,128)(2,1)S(1)} %bitcast.10) | data formatting | bytes 1048576
  58.0 0.8 %copy.15 = bf16[256,8,128]{2,1,0:T(8,128)(2,1)} copy(bf16[256,8,128]{2,1,0:T(8,128)(2,1)S(1)} %bitcast.9) | data formatting | bytes 1048576
  58.8 0.8 %copy.16 = bf16[256,8,128]{2,1,0:T(8,128)(2,1)} copy(bf16[256,8,128]{2,1,0:T(8,128)(2,1)S(1)} %bitcast.8) | data formatting | bytes 1048576
Async XLA Ops:
  0.6 0.7 %copy-start.4 = (s32[3,256]{1,0:T(4,128)S(1)}, s32[3,256]{1,0:T(4,128)}, u32[]{:S(2)}) copy-start(s32[3,256]{1,0:T(4,128)} %spans_ref.1) | copy-start | bytes 9220
  1.3 1.0 %copy-start = (bf16[256,8,128]{2,1,0:T(8,128)(2,1)S(1)}, bf16[256,8,128]{2,1,0:T(8,128)(2,1)}, u32[]{:S(2)}) copy-start(bf16[256,8,128]{2,1,0:T(8,128)(2,1)} %param.6) | copy-start | bytes 1572868
  2.4 1.0 %copy-start.1 = (bf16[256,8,128]{2,1,0:T(8,128)(2,1)S(1)}, bf16[256,8,128]{2,1,0:T(8,128)(2,1)}, u32[]{:S(2)}) copy-start(bf16[256,8,128]{2,1,0:T(8,128)(2,1)} %param.7) | copy-start | bytes 1572868
  3.4 1.0 %copy-start.2 = (bf16[256,8,128]{2,1,0:T(8,128)(2,1)S(1)}, bf16[256,8,128]{2,1,0:T(8,128)(2,1)}, u32[]{:S(2)}) copy-start(bf16[256,8,128]{2,1,0:T(8,128)(2,1)} %param.5) | copy-start | bytes 1572868
  4.4 1.0 %copy-start.3 = (bf16[256,8,128]{2,1,0:T(8,128)(2,1)S(1)}, bf16[256,8,128]{2,1,0:T(8,128)(2,1)}, u32[]{:S(2)}) copy-start(bf16[256,8,128]{2,1,0:T(8,128)(2,1)} %param.8) | copy-start | bytes 1572868

commit v3 on v2

--- a/solution.py
+++ b/solution.py
@@ -9,6 +9,7 @@
 from jax.sharding import PartitionSpec as P
 
 NEG = -1e30
+PIECES = 2
 MESH = pl.DeviceIdType.MESH
 F32 = jnp.float32
 BF16 = jnp.bfloat16
@@ -30,8 +31,8 @@
     count, tok, half, head_size,
     key_ref, value_ref, query_ref, grad_ref, spans_ref,
     att_out, query_out, key_out, value_out,
-    arg_ref, stage, od_in, last_in, kv, qd, span_own, span_other, bias, s_buf, dp_buf, grads, halo_out, halo_back, od, last,
-    span_sem, kv_sem, qd_sem, own_sem, fwd_sem, back_sem, od_sem, last_sem,
+    flat, spans_in, arg_ref, stage, od_in, last_in, kv, qd, span_own, span_other, bias, s_buf, dp_buf, grads, halo_out, halo_back, od, last,
+    load_sem, span_load_sem, span_sem, kv_sem, qd_sem, own_sem, fwd_sem, back_sem, od_sem, last_sem,
 ):
     me = lax.axis_index("seq")
     x = lax.rem(me, 2)
@@ -92,16 +93,15 @@
     def land_fwd(i):
         return remote(arg_ref.at[0, pl.ds(0, 2)], kv.at[i, :, other], fwd_sem, (i,), partner)
 
-    def land_back(i, block):
-        return send_back(i, block)
-
     rows = 2 * half * tok
 
     def head_rows(which, head):
         return pl.ds(which * rows + head, tok, stride=2 * half)
 
-    def pack(which, ref):
-        stage[which * rows : (which + 1) * rows, :] = ref[...].astype(F32)
+    def pack(which):
+        for piece in range(PIECES):
+            load(which, piece).wait()
+        stage[which * rows : (which + 1) * rows, :] = flat[which].astype(F32)
         for head in range(2 * half):
             arg_ref[head, which] = stage[head_rows(which, head), :].astype(BF16)
 
@@ -111,6 +111,20 @@
     def write(which, ref):
         ref[...] = stage[which * rows : (which + 1) * rows, :].astype(BF16)
 
+    inputs = (key_ref, value_ref, query_ref, grad_ref)
+
+    def load(which, piece):
+        at = pl.ds(piece * (rows // PIECES), rows // PIECES)
+        return pltpu.make_async_copy(
+            inputs[which].at[at], flat.at[which, at], load_sem.at[which, piece]
+        )
+
+    load_spans = pltpu.make_async_copy(spans_ref, spans_in, span_load_sem)
+    for which in range(4):
+        for piece in range(PIECES):
+            load(which, piece).start()
+    load_spans.start()
+
     barrier = pltpu.get_barrier_semaphore()
     pl.semaphore_signal(barrier, inc=1, device_id={"seq": partner}, device_id_type=MESH)
 
@@ -123,24 +137,25 @@
         pl.semaphore_signal(barrier, inc=1, device_id={"seq": me - 2}, device_id_type=MESH)
 
     span_own[...] = jnp.zeros_like(span_own)
-    span_own[0:3, :] = spans_ref[...]
-    pack(0, key_ref)
-    pack(1, value_ref)
+    pack(0)
+    pack(1)
+    load_spans.wait()
+    span_own[0:3, :] = spans_in[...]
     pl.semaphore_wait(barrier, 1 + has_next.astype(jnp.int32) + has_prev.astype(jnp.int32))
 
+    send_kv(0).start()
+
+    @pl.when(has_next)
+    def _():
+        send_own(0).start()
+        send_own(1).start()
+
     send_spans().start()
-    for i in range(half):
-        send_kv(i).start()
-
-    @pl.when(has_next)
-    def _():
-        for i in range(half):
-            send_own(i).start()
-
-    pack(2, query_ref)
-    pack(3, grad_ref)
-    for i in range(half):
-        send_qd(i).start()
+    pack(2)
+    pack(3)
+    send_qd(0).start()
+    send_kv(1).start()
+    send_qd(1).start()
 
     @pl.when(jnp.logical_not(has_prev))
     def _():
@@ -211,30 +226,42 @@
                 grads[i, at, 1] = value_part
             od[i, block, 1] = (query_grad * score_scale).T.astype(BF16)
 
+    def total(i, block):
+        return (grads[i, 2 + block] + halo_back[i, block].astype(F32)).astype(BF16)
+
     def finish(i):
         @pl.when(has_next)
         def _():
-            land_back(i, other).wait_recv()
-
-        last[i] = (grads[i, 2 + other] + halo_back[i, other].astype(F32)).astype(BF16)
+            send_back(i, other).wait_recv()
+
+        last[i] = total(i, other)
         send_last(i).start()
 
+    def forward(i):
+        land_kv(i).wait_recv()
+
         @pl.when(has_next)
         def _():
-            land_back(i, x).wait_recv()
-
-        done = grads[i, 2 + x] + halo_back[i, x].astype(F32)
-        for which in range(2):
-            unpack(2 + which, x * half + i, done[which])
+            send_fwd(i).start()
 
     def step(i, carry):
-        land_kv(i).wait_recv()
-
-        @pl.when(has_next)
-        def _():
-            send_fwd(i).start()
-
         land_qd(i).wait_recv()
+
+        @pl.when(i + 2 < half)
+        def _():
+            send_kv(i + 2).start()
+
+        @pl.when(i + 1 < half)
+        def _():
+            forward(i + 1)
+
+        @pl.when(i + 2 < half)
+        def _():
+            send_qd(i + 2).start()
+
+            @pl.when(has_next)
+            def _():
+                send_own(i + 2).start()
 
         @pl.when(has_prev)
         def _():
@@ -259,10 +286,18 @@
 
         return carry
 
+    forward(0)
     lax.fori_loop(0, half, step, 0)
     finish(half - 1)
 
     for i in range(half):
+        @pl.when(has_next)
+        def _():
+            send_back(i, x).wait_recv()
+
+        done = total(i, x)
+        for which in range(2):
+            unpack(2 + which, x * half + i, done[which])
         send_od(i).wait_recv()
         for which in range(2):
             unpack(which, other * half + i, od_in[i, which])
@@ -295,6 +330,22 @@
             send_back(i, x).wait_send()
 
 
+def writer(att_ref, query_ref, key_ref, value_ref, att_out, query_out, key_out, value_out, sems):
+    pairs = (
+        (att_ref, att_out), (query_ref, query_out), (key_ref, key_out), (value_ref, value_out)
+    )
+    copies = []
+    for which, (src, dst) in enumerate(pairs):
+        rows = src.shape[0] // PIECES
+        for piece in range(PIECES):
+            at = pl.ds(piece * rows, rows)
+            copies.append(pltpu.make_async_copy(src.at[at], dst.at[at], sems.at[which, piece]))
+    for copy in copies:
+        copy.start()
+    for copy in copies:
+        copy.wait()
+
+
 def per_device(count, queries, keys, values, out_grad, spans):
     tok, heads, head_size = queries.shape
     half = heads // 2
@@ -305,9 +356,11 @@
     out = pl.pallas_call(
         functools.partial(kernel, count, tok, half, head_size),
         out_shape=[jax.ShapeDtypeStruct((tok * heads, head_size), BF16)] * 4,
-        in_specs=[pl.BlockSpec(memory_space=vmem)] * 5,
+        in_specs=[pl.BlockSpec(memory_space=pltpu.HBM)] * 5,
         out_specs=[pl.BlockSpec(memory_space=vmem)] * 4,
         scratch_shapes=[
+            vmem((4, heads * tok, head_size), BF16),
+            vmem(spans.shape, jnp.int32),
             vmem((heads, 4, tok, head_size), BF16),
             vmem((4 * heads * tok, head_size), F32),
             vmem((half, 2, tok, head_size), BF16),
@@ -324,6 +377,8 @@
             vmem((half, 2, 2, tok, head_size), BF16),
             vmem((half, 2, 2, tok, head_size), BF16),
             vmem((half, 2, tok, head_size), BF16),
+            dma((4, PIECES)),
+            dma,
             dma((2,)),
             dma((2, half)),
             dma((2, half)),
@@ -334,14 +389,21 @@
             dma((2, half)),
         ],
         compiler_params=pltpu.CompilerParams(
-            collective_id=0, has_side_effects=True, vmem_limit_bytes=48 * 1024 * 1024
+            collective_id=0, has_side_effects=True, vmem_limit_bytes=52736 * 1024
         ),
         cost_estimate=pl.CostEstimate(
             flops=blocks * 12 * tok * tok * head_size,
-            bytes_accessed=16 * heads * tok * head_size,
+            bytes_accessed=8 * heads * tok * head_size,
             transcendentals=blocks * tok * tok,
         ),
     )(*flat, spans)
+    out = pl.pallas_call(
+        writer,
+        out_shape=[jax.ShapeDtypeStruct((tok * heads, head_size), BF16)] * 4,
+        in_specs=[pl.BlockSpec(memory_space=vmem)] * 4,
+        out_specs=[pl.BlockSpec(memory_space=pltpu.HBM)] * 4,
+        scratch_shapes=[dma((4, PIECES))],
+    )(*out)
     return tuple(a.reshape(tok, heads, head_size) for a in out)
 
 

time: 60 us -> 58.8 us (0.980)
  local copies, waits for them, and re-layouts: 8.02 us -> 3.86 us
  Pallas kernels: 51 us -> 54.1 us
    unnamed x14 -> x10, local copies, waits for them, and re-layouts: 8.02 us -> 3.86 us
    pallas_call x0 -> x1, Pallas kernels: none -> 2.89 us  [per_device(): pl.pallas_call(writer, out_shape=[jax.ShapeDtypeStruct((tok * heads, head...]
where the time goes in v3:
time: 58.8 us; the launch traced here: 58.6 us
  Pallas kernels  54.1 us (92%)
  local copies, waits for them, and re-layouts  3.86 us (7%)
  between operations  0.66 us (1%)
    pallas_call x1, Pallas kernels, per_device(): pl.pallas_call(functools.partial(kernel, count, tok, half, head_size), ou...  51.2 us
    unnamed x10, local copies, waits for them, and re-layouts  3.86 us
    pallas_call x1, Pallas kernels, per_device(): pl.pallas_call(writer, out_shape=[jax.ShapeDtypeStruct((tok * heads, head...  2.89 us

profile of v3, /device:TPU:0, one launch (start us, length us, event | category | flops | bytes accessed | tf_op | source)
XLA Modules:
  0.0 58.6 jit_solution(14385325660336440057)
XLA Ops:
  0.6 0.0 copy-start.4
  0.6 0.7 %copy-done.4 = s32[3,256]{1,0:T(4,128)S(1)} copy-done((s32[3,256]{1,0:T(4,128)S(1)}, s32[3,256]{1,0:T(4,128)}, u32[]{:S(2)}) %copy-start.4) | copy-done | bytes 3096
  1.3 51.2 %shard_map.84 = (bf16[2048,128]{1,0:T(8,128)(2,1)S(1)}, bf16[2048,128]{1,0:T(8,128)(2,1)S(1)}, bf16[2048,128]{1,0:T(8,128)(2,1)S(1)}, bf16[2048,128]{1,0:T(8,128)(2,1)S(1)}) custom-call(bf16[2048,128]{1,0:T(8,128)(2,1)} %bitcast.8, bf16[2048,128]{1,0:T(8,128)(2,1)} %bitcast.9, bf16[2048,128]{1,0:T(8,128)(2,1)} %bitcast.10, bf16[2048,128]{1,0:T(8,128)(2,1)} %bitcast.11, ...), custom_call_target="tpu_custom_call" | custom-call | flops 2415919104 | bytes 2097152 | tf_op jit(solution)/shard_map/pallas_call | solution.py:356
  52.6 0.0 copy-start
  52.6 0.8 %copy-done = bf16[2048,128]{1,0:T(8,128)(2,1)} copy-done((bf16[2048,128]{1,0:T(8,128)(2,1)}, bf16[2048,128]{1,0:T(8,128)(2,1)S(1)}, u32[]{:S(2)}) %copy-start) | copy-done | bytes 524312
  53.4 0.0 copy-start.1
  53.4 0.8 %copy-done.1 = bf16[2048,128]{1,0:T(8,128)(2,1)} copy-done((bf16[2048,128]{1,0:T(8,128)(2,1)}, bf16[2048,128]{1,0:T(8,128)(2,1)S(1)}, u32[]{:S(2)}) %copy-start.1) | copy-done | bytes 524312
  54.1 0.0 copy-start.2
  54.2 0.8 %copy-done.2 = bf16[2048,128]{1,0:T(8,128)(2,1)} copy-done((bf16[2048,128]{1,0:T(8,128)(2,1)}, bf16[2048,128]{1,0:T(8,128)(2,1)S(1)}, u32[]{:S(2)}) %copy-start.2) | copy-done | bytes 524312
  55.0 0.0 copy-start.3
  55.0 0.8 %copy-done.3 = bf16[2048,128]{1,0:T(8,128)(2,1)} copy-done((bf16[2048,128]{1,0:T(8,128)(2,1)}, bf16[2048,128]{1,0:T(8,128)(2,1)S(1)}, u32[]{:S(2)}) %copy-start.3) | copy-done | bytes 524312
  55.8 2.9 %shard_map.85 = (bf16[2048,128]{1,0:T(8,128)(2,1)}, bf16[2048,128]{1,0:T(8,128)(2,1)}, bf16[2048,128]{1,0:T(8,128)(2,1)}, bf16[2048,128]{1,0:T(8,128)(2,1)}) custom-call(bf16[2048,128]{1,0:T(8,128)(2,1)} %copy-done, bf16[2048,128]{1,0:T(8,128)(2,1)} %copy-done.1, bf16[2048,128]{1,0:T(8,128)(2,1)} %copy-done.2, bf16[2048,128]{1,0:T(8,128)(2,1)} %copy-done.3), custom_call_target="tpu_custom_call" | custom-call | tf_op jit(solution)/shard_map/pallas_call | solution.py:400
Async XLA Ops:
  0.6 0.7 %copy-start.4 = (s32[3,256]{1,0:T(4,128)S(1)}, s32[3,256]{1,0:T(4,128)}, u32[]{:S(2)}) copy-start(s32[3,256]{1,0:T(4,128)} %spans_ref.1) | copy-start | bytes 9220
  52.6 0.8 %copy-start = (bf16[2048,128]{1,0:T(8,128)(2,1)}, bf16[2048,128]{1,0:T(8,128)(2,1)S(1)}, u32[]{:S(2)}) copy-start(bf16[2048,128]{1,0:T(8,128)(2,1)S(1)} %get-tuple-element.12.att_ref) | copy-start | bytes 1572868
  53.4 0.8 %copy-start.1 = (bf16[2048,128]{1,0:T(8,128)(2,1)}, bf16[2048,128]{1,0:T(8,128)(2,1)S(1)}, u32[]{:S(2)}) copy-start(bf16[2048,128]{1,0:T(8,128)(2,1)S(1)} %get-tuple-element.13.query_ref) | copy-start | bytes 1572868
  54.1 0.8 %copy-start.2 = (bf16[2048,128]{1,0:T(8,128)(2,1)}, bf16[2048,128]{1,0:T(8,128)(2,1)S(1)}, u32[]{:S(2)}) copy-start(bf16[2048,128]{1,0:T(8,128)(2,1)S(1)} %get-tuple-element.14.key_ref) | copy-start | bytes 1572868
  55.0 0.8 %copy-start.3 = (bf16[2048,128]{1,0:T(8,128)(2,1)}, bf16[2048,128]{1,0:T(8,128)(2,1)S(1)}, u32[]{:S(2)}) copy-start(bf16[2048,128]{1,0:T(8,128)(2,1)S(1)} %get-tuple-element.15.value_ref) | copy-start | bytes 1572868

commit v4 on v3

--- a/solution.py
+++ b/solution.py
@@ -330,22 +330,6 @@
             send_back(i, x).wait_send()
 
 
-def writer(att_ref, query_ref, key_ref, value_ref, att_out, query_out, key_out, value_out, sems):
-    pairs = (
-        (att_ref, att_out), (query_ref, query_out), (key_ref, key_out), (value_ref, value_out)
-    )
-    copies = []
-    for which, (src, dst) in enumerate(pairs):
-        rows = src.shape[0] // PIECES
-        for piece in range(PIECES):
-            at = pl.ds(piece * rows, rows)
-            copies.append(pltpu.make_async_copy(src.at[at], dst.at[at], sems.at[which, piece]))
-    for copy in copies:
-        copy.start()
-    for copy in copies:
-        copy.wait()
-
-
 def per_device(count, queries, keys, values, out_grad, spans):
     tok, heads, head_size = queries.shape
     half = heads // 2
@@ -355,7 +339,7 @@
     blocks = 3 * 2 * heads // 2
     out = pl.pallas_call(
         functools.partial(kernel, count, tok, half, head_size),
-        out_shape=[jax.ShapeDtypeStruct((tok * heads, head_size), BF16)] * 4,
+        out_shape=[vmem((tok * heads, head_size), BF16)] * 4,
         in_specs=[pl.BlockSpec(memory_space=pltpu.HBM)] * 5,
         out_specs=[pl.BlockSpec(memory_space=vmem)] * 4,
         scratch_shapes=[
@@ -389,21 +373,14 @@
             dma((2, half)),
         ],
         compiler_params=pltpu.CompilerParams(
-            collective_id=0, has_side_effects=True, vmem_limit_bytes=52736 * 1024
+            collective_id=0, has_side_effects=True, vmem_limit_bytes=48 * 1024 * 1024
         ),
         cost_estimate=pl.CostEstimate(
             flops=blocks * 12 * tok * tok * head_size,
             bytes_accessed=8 * heads * tok * head_size,
             transcendentals=blocks * tok * tok,
         ),
-    )(*flat, spans)
-    out = pl.pallas_call(
-        writer,
-        out_shape=[jax.ShapeDtypeStruct((tok * heads, head_size), BF16)] * 4,
-        in_specs=[pl.BlockSpec(memory_space=vmem)] * 4,
-        out_specs=[pl.BlockSpec(memory_space=pltpu.HBM)] * 4,
-        scratch_shapes=[dma((4, PIECES))],
-    )(*out)
+    )(*[pltpu.with_memory_space_constraint(a, pltpu.HBM) for a in (*flat, spans)])
     return tuple(a.reshape(tok, heads, head_size) for a in out)
 
 

time: 58.8 us -> 55.2 us (0.939)
  Pallas kernels: 54.1 us -> 51.3 us
  local copies, waits for them, and re-layouts: 3.86 us -> 3.17 us
    pallas_call x1 -> x0, Pallas kernels: 2.89 us -> none  [per_device(): pl.pallas_call(writer, out_shape=[jax.ShapeDtypeStruct((tok * heads, head...]
    unnamed x10 -> x4, local copies, waits for them, and re-layouts: 3.86 us -> 3.17 us
where the time goes in v4:
time: 55.2 us; the launch traced here: 55.1 us
  Pallas kernels  51.3 us (93%)
  local copies, waits for them, and re-layouts  3.17 us (6%)
  between operations  0.64 us (1%)
    pallas_call x1, Pallas kernels, per_device(): pl.pallas_call(functools.partial(kernel, count, tok, half, head_size), ou...  51.3 us
    unnamed x4, local copies, waits for them, and re-layouts  3.17 us

profile of v4, /device:TPU:0, one launch (start us, length us, event | category | flops | bytes accessed | tf_op | source)
XLA Modules:
  0.0 55.1 jit_solution(14499286542155469067)
XLA Ops:
  0.6 51.3 %shard_map.84 = (bf16[2048,128]{1,0:T(8,128)(2,1)S(1)}, bf16[2048,128]{1,0:T(8,128)(2,1)S(1)}, bf16[2048,128]{1,0:T(8,128)(2,1)S(1)}, bf16[2048,128]{1,0:T(8,128)(2,1)S(1)}) custom-call(bf16[2048,128]{1,0:T(8,128)(2,1)} %bitcast.12, bf16[2048,128]{1,0:T(8,128)(2,1)} %bitcast.13, bf16[2048,128]{1,0:T(8,128)(2,1)} %bitcast.14, bf16[2048,128]{1,0:T(8,128)(2,1)} %bitcast.15, ...), custom_call_target="tpu_custom_call" | custom-call | flops 2415919104 | bytes 2097152 | tf_op jit(solution)/shard_map/pallas_call | solution.py:340
  51.9 0.8 %copy.13 = bf16[256,8,128]{2,1,0:T(8,128)(2,1)} copy(bf16[256,8,128]{2,1,0:T(8,128)(2,1)S(1)} %bitcast.11) | data formatting | bytes 1048576
  52.7 0.8 %copy.14 = bf16[256,8,128]{2,1,0:T(8,128)(2,1)} copy(bf16[256,8,128]{2,1,0:T(8,128)(2,1)S(1)} %bitcast.10) | data formatting | bytes 1048576
  53.5 0.8 %copy.15 = bf16[256,8,128]{2,1,0:T(8,128)(2,1)} copy(bf16[256,8,128]{2,1,0:T(8,128)(2,1)S(1)} %bitcast.9) | data formatting | bytes 1048576
  54.3 0.8 %copy.16 = bf16[256,8,128]{2,1,0:T(8,128)(2,1)} copy(bf16[256,8,128]{2,1,0:T(8,128)(2,1)S(1)} %bitcast.8) | data formatting | bytes 1048576

commit v5 on v4

--- a/solution.py
+++ b/solution.py
@@ -98,12 +98,13 @@
     def head_rows(which, head):
         return pl.ds(which * rows + head, tok, stride=2 * half)
 
-    def pack(which):
-        for piece in range(PIECES):
-            load(which, piece).wait()
-        stage[which * rows : (which + 1) * rows, :] = flat[which].astype(F32)
+    def pack(which, piece):
+        span, part = rows // PIECES, tok // PIECES
+        low = which * rows + piece * span
+        stage[low : low + span, :] = flat[which, piece * span : (piece + 1) * span].astype(F32)
         for head in range(2 * half):
-            arg_ref[head, which] = stage[head_rows(which, head), :].astype(BF16)
+            block = stage[pl.ds(low + head, part, stride=2 * half), :]
+            arg_ref[head, which, piece * part : (piece + 1) * part] = block.astype(BF16)
 
     def unpack(which, head, block):
         stage[head_rows(which, head), :] = block.astype(F32)
@@ -120,9 +121,9 @@
         )
 
     load_spans = pltpu.make_async_copy(spans_ref, spans_in, span_load_sem)
-    for which in range(4):
-        for piece in range(PIECES):
-            load(which, piece).start()
+    for piece in range(PIECES):
+        load(0, piece).start()
+        load(1, piece).start()
     load_spans.start()
 
     barrier = pltpu.get_barrier_semaphore()
@@ -137,8 +138,15 @@
         pl.semaphore_signal(barrier, inc=1, device_id={"seq": me - 2}, device_id_type=MESH)
 
     span_own[...] = jnp.zeros_like(span_own)
-    pack(0)
-    pack(1)
+    for piece in range(PIECES):
+        load(0, piece).wait()
+        load(1, piece).wait()
+        if piece == PIECES - 1:
+            for later in range(PIECES):
+                load(2, later).start()
+                load(3, later).start()
+        pack(0, piece)
+        pack(1, piece)
     load_spans.wait()
     span_own[0:3, :] = spans_in[...]
     pl.semaphore_wait(barrier, 1 + has_next.astype(jnp.int32) + has_prev.astype(jnp.int32))
@@ -151,8 +159,11 @@
         send_own(1).start()
 
     send_spans().start()
-    pack(2)
-    pack(3)
+    for piece in range(PIECES):
+        load(2, piece).wait()
+        load(3, piece).wait()
+        pack(2, piece)
+        pack(3, piece)
     send_qd(0).start()
     send_kv(1).start()
     send_qd(1).start()
@@ -268,6 +279,10 @@
             land_own(i).wait_recv()
             land_fwd(i).wait_recv()
 
+        @pl.when(i == half - 2)
+        def _():
+            send_od(0).start()
+
         compute(i)
 
         @pl.when(has_prev)
@@ -276,14 +291,20 @@
             send_back(i, other).start()
             send_back(i, x).start()
 
-        send_od(i).start()
+        @pl.when(i == half - 2)
+        def _():
+            for done in range(1, half - 1):
+                send_od(done).start()
+            for done in range(half - 2):
+                finish(done)
+
+        @pl.when(i == half - 1)
+        def _():
+            send_od(half - 1).start()
+            finish(half - 2)
+
         for which in range(2):
             unpack(which, x * half + i, od[i, x, which])
-
-        @pl.when(i > 0)
-        def _():
-            finish(i - 1)
-
         return carry
 
     forward(0)

time: 55.2 us -> 55.2 us (level)
  no operation moved by 1% of the time
where the time goes in v5:
time: 55.2 us; the launch traced here: 55.1 us
  Pallas kernels  51.2 us (93%)
  local copies, waits for them, and re-layouts  3.17 us (6%)
  between operations  0.64 us (1%)
    pallas_call x1, Pallas kernels, per_device(): pl.pallas_call(functools.partial(kernel, count, tok, half, head_size), ou...  51.2 us
    unnamed x4, local copies, waits for them, and re-layouts  3.17 us

profile of v5, /device:TPU:0, one launch (start us, length us, event | category | flops | bytes accessed | tf_op | source)
XLA Modules:
  0.0 55.1 jit_solution(5407671614795367399)
XLA Ops:
  0.6 51.2 %shard_map.84 = (bf16[2048,128]{1,0:T(8,128)(2,1)S(1)}, bf16[2048,128]{1,0:T(8,128)(2,1)S(1)}, bf16[2048,128]{1,0:T(8,128)(2,1)S(1)}, bf16[2048,128]{1,0:T(8,128)(2,1)S(1)}) custom-call(bf16[2048,128]{1,0:T(8,128)(2,1)} %bitcast.12, bf16[2048,128]{1,0:T(8,128)(2,1)} %bitcast.13, bf16[2048,128]{1,0:T(8,128)(2,1)} %bitcast.14, bf16[2048,128]{1,0:T(8,128)(2,1)} %bitcast.15, ...), custom_call_target="tpu_custom_call" | custom-call | flops 2415919104 | bytes 2097152 | tf_op jit(solution)/shard_map/pallas_call | solution.py:361
  51.9 0.8 %copy.13 = bf16[256,8,128]{2,1,0:T(8,128)(2,1)} copy(bf16[256,8,128]{2,1,0:T(8,128)(2,1)S(1)} %bitcast.11) | data formatting | bytes 1048576
  52.7 0.8 %copy.14 = bf16[256,8,128]{2,1,0:T(8,128)(2,1)} copy(bf16[256,8,128]{2,1,0:T(8,128)(2,1)S(1)} %bitcast.10) | data formatting | bytes 1048576
  53.5 0.8 %copy.15 = bf16[256,8,128]{2,1,0:T(8,128)(2,1)} copy(bf16[256,8,128]{2,1,0:T(8,128)(2,1)S(1)} %bitcast.9) | data formatting | bytes 1048576
  54.3 0.8 %copy.16 = bf16[256,8,128]{2,1,0:T(8,128)(2,1)} copy(bf16[256,8,128]{2,1,0:T(8,128)(2,1)S(1)} %bitcast.8) | data formatting | bytes 1048576

commit v6 on v5

--- a/solution.py
+++ b/solution.py
@@ -30,7 +30,7 @@
 def kernel(
     count, tok, half, head_size,
     key_ref, value_ref, query_ref, grad_ref, spans_ref,
-    att_out, query_out, key_out, value_out,
+    out_ref,
     flat, spans_in, arg_ref, stage, od_in, last_in, kv, qd, span_own, span_other, bias, s_buf, dp_buf, grads, halo_out, halo_back, od, last,
     load_sem, span_load_sem, span_sem, kv_sem, qd_sem, own_sem, fwd_sem, back_sem, od_sem, last_sem,
 ):
@@ -56,9 +56,9 @@
     def send_spans():
         return remote(span_own, span_other, span_sem, (), partner)
 
-    def send_kv(i):
-        src = arg_ref.at[other * half + i, pl.ds(0, 2)]
-        return remote(src, kv.at[i, :, 2 + x], kv_sem, (i,), partner)
+    def send_kv(i, which):
+        src = arg_ref.at[other * half + i, which]
+        return remote(src, kv.at[i, which, 2 + x], kv_sem, (i, which), partner)
 
     def send_qd(i):
         src = arg_ref.at[other * half + i, pl.ds(2, 2)]
@@ -80,9 +80,9 @@
     def send_last(i):
         return remote(last.at[i], last_in.at[i], last_sem, (i,), partner)
 
-    def land_kv(i):
-        dst = kv.at[i, :, 2 + other]
-        return remote(arg_ref.at[0, pl.ds(0, 2)], dst, kv_sem, (i,), partner)
+    def land_kv(i, which):
+        dst = kv.at[i, which, 2 + other]
+        return remote(arg_ref.at[0, which], dst, kv_sem, (i, which), partner)
 
     def land_qd(i):
         return remote(arg_ref.at[0, pl.ds(2, 2)], qd.at[i, other], qd_sem, (i,), partner)
@@ -109,8 +109,8 @@
     def unpack(which, head, block):
         stage[head_rows(which, head), :] = block.astype(F32)
 
-    def write(which, ref):
-        ref[...] = stage[which * rows : (which + 1) * rows, :].astype(BF16)
+    def write(which):
+        out_ref[which] = stage[which * rows : (which + 1) * rows, :].astype(BF16)
 
     inputs = (key_ref, value_ref, query_ref, grad_ref)
 
@@ -123,6 +123,7 @@
     load_spans = pltpu.make_async_copy(spans_ref, spans_in, span_load_sem)
     for piece in range(PIECES):
         load(0, piece).start()
+    for piece in range(PIECES):
         load(1, piece).start()
     load_spans.start()
 
@@ -137,35 +138,38 @@
     def _():
         pl.semaphore_signal(barrier, inc=1, device_id={"seq": me - 2}, device_id_type=MESH)
 
-    span_own[...] = jnp.zeros_like(span_own)
     for piece in range(PIECES):
         load(0, piece).wait()
+        pack(0, piece)
+    pl.semaphore_wait(barrier, 1 + has_next.astype(jnp.int32) + has_prev.astype(jnp.int32))
+    send_kv(0, 0).start()
+    send_kv(1, 0).start()
+
+    for which in (2, 3):
+        for piece in range(PIECES):
+            load(which, piece).start()
+    for piece in range(PIECES):
         load(1, piece).wait()
-        if piece == PIECES - 1:
-            for later in range(PIECES):
-                load(2, later).start()
-                load(3, later).start()
-        pack(0, piece)
         pack(1, piece)
-    load_spans.wait()
-    span_own[0:3, :] = spans_in[...]
-    pl.semaphore_wait(barrier, 1 + has_next.astype(jnp.int32) + has_prev.astype(jnp.int32))
-
-    send_kv(0).start()
+    send_kv(0, 1).start()
+    send_kv(1, 1).start()
 
     @pl.when(has_next)
     def _():
         send_own(0).start()
         send_own(1).start()
 
+    load_spans.wait()
+    span_own[...] = jnp.zeros_like(span_own)
+    span_own[0:3, :] = spans_in[...]
     send_spans().start()
     for piece in range(PIECES):
         load(2, piece).wait()
+        pack(2, piece)
+    for piece in range(PIECES):
         load(3, piece).wait()
-        pack(2, piece)
         pack(3, piece)
     send_qd(0).start()
-    send_kv(1).start()
     send_qd(1).start()
 
     @pl.when(jnp.logical_not(has_prev))
@@ -249,7 +253,8 @@
         send_last(i).start()
 
     def forward(i):
-        land_kv(i).wait_recv()
+        land_kv(i, 0).wait_recv()
+        land_kv(i, 1).wait_recv()
 
         @pl.when(has_next)
         def _():
@@ -260,7 +265,8 @@
 
         @pl.when(i + 2 < half)
         def _():
-            send_kv(i + 2).start()
+            send_kv(i + 2, 0).start()
+            send_kv(i + 2, 1).start()
 
         @pl.when(i + 1 < half)
         def _():
@@ -323,17 +329,18 @@
         for which in range(2):
             unpack(which, other * half + i, od_in[i, which])
         if i == half - 1:
-            write(0, att_out)
-            write(1, query_out)
+            write(0)
+            write(1)
         send_last(i).wait_recv()
         for which in range(2):
             unpack(2 + which, other * half + i, last_in[i, which])
-    write(2, key_out)
-    write(3, value_out)
+    write(2)
+    write(3)
 
     send_spans().wait_send()
     for i in range(half):
-        send_kv(i).wait_send()
+        send_kv(i, 0).wait_send()
+        send_kv(i, 1).wait_send()
         send_qd(i).wait_send()
         send_od(i).wait_send()
         send_last(i).wait_send()
@@ -360,9 +367,9 @@
     blocks = 3 * 2 * heads // 2
     out = pl.pallas_call(
         functools.partial(kernel, count, tok, half, head_size),
-        out_shape=[vmem((tok * heads, head_size), BF16)] * 4,
+        out_shape=vmem((4, tok * heads, head_size), BF16),
         in_specs=[pl.BlockSpec(memory_space=pltpu.HBM)] * 5,
-        out_specs=[pl.BlockSpec(memory_space=vmem)] * 4,
+        out_specs=pl.BlockSpec(memory_space=vmem),
         scratch_shapes=[
             vmem((4, heads * tok, head_size), BF16),
             vmem(spans.shape, jnp.int32),
@@ -385,7 +392,7 @@
             dma((4, PIECES)),
             dma,
             dma((2,)),
-            dma((2, half)),
+            dma((2, half, 2)),
             dma((2, half)),
             dma((2, half)),
             dma((2, half)),
@@ -402,7 +409,7 @@
             transcendentals=blocks * tok * tok,
         ),
     )(*[pltpu.with_memory_space_constraint(a, pltpu.HBM) for a in (*flat, spans)])
-    return tuple(a.reshape(tok, heads, head_size) for a in out)
+    return tuple(out[r].reshape(tok, heads, head_size) for r in range(4))
 
 
 def solution(mesh):

time: 55.2 us -> 53.3 us (0.966)
  local copies, waits for them, and re-layouts: 3.17 us -> 1.35 us
    unnamed x4 -> x0, local copies, waits for them, and re-layouts: 3.17 us -> none
    another operation x0 -> x1, local copies, waits for them, and re-layouts: none -> 1.35 us  [per_device(): return tuple((out[r].reshape(tok, heads, head_size) for r in range(4)))]
where the time goes in v6:
time: 53.3 us; the launch traced here: 53.2 us
  Pallas kernels  51.2 us (96%)
  local copies, waits for them, and re-layouts  1.35 us (3%)
  between operations  0.64 us (1%)
    pallas_call x1, Pallas kernels, per_device(): pl.pallas_call(functools.partial(kernel, count, tok, half, head_size), ou...  51.2 us
    another operation x1, local copies, waits for them, and re-layouts, per_device(): return tuple((out[r].reshape(tok, heads, head_size) for r in range(4)))  1.35 us

profile of v6, /device:TPU:0, one launch (start us, length us, event | category | flops | bytes accessed | tf_op | source)
XLA Modules:
  0.0 53.2 jit_solution(10700971266169256934)
XLA Ops:
  0.6 51.2 %shard_map.84 = bf16[4,2048,128]{2,1,0:T(8,128)(2,1)S(1)} custom-call(bf16[2048,128]{1,0:T(8,128)(2,1)} %bitcast.12, bf16[2048,128]{1,0:T(8,128)(2,1)} %bitcast.13, bf16[2048,128]{1,0:T(8,128)(2,1)} %bitcast.14, bf16[2048,128]{1,0:T(8,128)(2,1)} %bitcast.15, s32[3,256]{1,0:T(4,128)} %spans_ref.1), custom_call_target="tpu_custom_call" | custom-call | flops 2415919104 | bytes 2097152 | tf_op jit(solution)/shard_map/pallas_call | solution.py:368
  51.8 1.3 %slice_bitcast_fusion = (bf16[256,8,128]{2,1,0:T(8,128)(2,1)}, bf16[256,8,128]{2,1,0:T(8,128)(2,1)}, bf16[256,8,128]{2,1,0:T(8,128)(2,1)}, bf16[256,8,128]{2,1,0:T(8,128)(2,1)}) fusion(bf16[4,2048,128]{2,1,0:T(8,128)(2,1)S(1)} %shard_map.84), kind=kLoop, calls=%fused_computation | loop fusion | bytes 4194304 | tf_op jit(solution)/shard_map/reshape;squeeze | solution.py:412

commit v7 on v6

--- a/solution.py
+++ b/solution.py
@@ -285,10 +285,6 @@
             land_own(i).wait_recv()
             land_fwd(i).wait_recv()
 
-        @pl.when(i == half - 2)
-        def _():
-            send_od(0).start()
-
         compute(i)
 
         @pl.when(has_prev)
@@ -297,17 +293,11 @@
             send_back(i, other).start()
             send_back(i, x).start()
 
-        @pl.when(i == half - 2)
-        def _():
-            for done in range(1, half - 1):
-                send_od(done).start()
-            for done in range(half - 2):
-                finish(done)
-
-        @pl.when(i == half - 1)
-        def _():
-            send_od(half - 1).start()
-            finish(half - 2)
+        send_od(i).start()
+
+        @pl.when(i > 0)
+        def _():
+            finish(i - 1)
 
         for which in range(2):
             unpack(which, x * half + i, od[i, x, which])

time: 53.3 us -> 53.3 us (level)
  no operation moved by 1% of the time
where the time goes in v7:
time: 53.3 us; the launch traced here: 53.2 us
  Pallas kernels  51.2 us (96%)
  local copies, waits for them, and re-layouts  1.35 us (3%)
  between operations  0.64 us (1%)
    pallas_call x1, Pallas kernels, per_device(): pl.pallas_call(functools.partial(kernel, count, tok, half, head_size), ou...  51.2 us
    another operation x1, local copies, waits for them, and re-layouts, per_device(): return tuple((out[r].reshape(tok, heads, head_size) for r in range(4)))  1.35 us

profile of v7, /device:TPU:0, one launch (start us, length us, event | category | flops | bytes accessed | tf_op | source)
XLA Modules:
  0.0 53.2 jit_solution(17862229558175837064)
XLA Ops:
  0.6 51.2 %shard_map.84 = bf16[4,2048,128]{2,1,0:T(8,128)(2,1)S(1)} custom-call(bf16[2048,128]{1,0:T(8,128)(2,1)} %bitcast.12, bf16[2048,128]{1,0:T(8,128)(2,1)} %bitcast.13, bf16[2048,128]{1,0:T(8,128)(2,1)} %bitcast.14, bf16[2048,128]{1,0:T(8,128)(2,1)} %bitcast.15, s32[3,256]{1,0:T(4,128)} %spans_ref.1), custom_call_target="tpu_custom_call" | custom-call | flops 2415919104 | bytes 2097152 | tf_op jit(solution)/shard_map/pallas_call | solution.py:358
  51.8 1.3 %slice_bitcast_fusion = (bf16[256,8,128]{2,1,0:T(8,128)(2,1)}, bf16[256,8,128]{2,1,0:T(8,128)(2,1)}, bf16[256,8,128]{2,1,0:T(8,128)(2,1)}, bf16[256,8,128]{2,1,0:T(8,128)(2,1)}) fusion(bf16[4,2048,128]{2,1,0:T(8,128)(2,1)S(1)} %shard_map.84), kind=kLoop, calls=%fused_computation | loop fusion | bytes 4194304 | tf_op jit(solution)/shard_map/reshape;squeeze | solution.py:402

commit v8 on v6

--- a/solution.py
+++ b/solution.py
@@ -9,7 +9,7 @@
 from jax.sharding import PartitionSpec as P
 
 NEG = -1e30
-PIECES = 2
+PIECES = 4
 MESH = pl.DeviceIdType.MESH
 F32 = jnp.float32
 BF16 = jnp.bfloat16

time: 53.3 us -> 53.4 us (level)
  no operation moved by 1% of the time
where the time goes in v8:
time: 53.4 us; the launch traced here: 53.2 us
  Pallas kernels  51.2 us (96%)
  local copies, waits for them, and re-layouts  1.35 us (3%)
  between operations  0.64 us (1%)
    pallas_call x1, Pallas kernels, per_device(): pl.pallas_call(functools.partial(kernel, count, tok, half, head_size), ou...  51.2 us
    another operation x1, local copies, waits for them, and re-layouts, per_device(): return tuple((out[r].reshape(tok, heads, head_size) for r in range(4)))  1.35 us

profile of v8, /device:TPU:0, one launch (start us, length us, event | category | flops | bytes accessed | tf_op | source)
XLA Modules:
  0.0 53.2 jit_solution(14958054887380076103)
XLA Ops:
  0.6 51.2 %shard_map.84 = bf16[4,2048,128]{2,1,0:T(8,128)(2,1)S(1)} custom-call(bf16[2048,128]{1,0:T(8,128)(2,1)} %bitcast.12, bf16[2048,128]{1,0:T(8,128)(2,1)} %bitcast.13, bf16[2048,128]{1,0:T(8,128)(2,1)} %bitcast.14, bf16[2048,128]{1,0:T(8,128)(2,1)} %bitcast.15, s32[3,256]{1,0:T(4,128)} %spans_ref.1), custom_call_target="tpu_custom_call" | custom-call | flops 2415919104 | bytes 2097152 | tf_op jit(solution)/shard_map/pallas_call | solution.py:368
  51.9 1.3 %slice_bitcast_fusion = (bf16[256,8,128]{2,1,0:T(8,128)(2,1)}, bf16[256,8,128]{2,1,0:T(8,128)(2,1)}, bf16[256,8,128]{2,1,0:T(8,128)(2,1)}, bf16[256,8,128]{2,1,0:T(8,128)(2,1)}) fusion(bf16[4,2048,128]{2,1,0:T(8,128)(2,1)S(1)} %shard_map.84), kind=kLoop, calls=%fused_computation | loop fusion | bytes 4194304 | tf_op jit(solution)/shard_map/reshape;squeeze | solution.py:412
